TPU v7x, 32 devices: a whole 2x2x4 slice. The times are simulated.
32 devices in a mesh: section: 4 (over x, core), dp: 8 (over z, y).
Axes of the slice: x: 2, y: 2, z: 4, core: 2. Of those that a mesh axis runs over, the one named last changes fastest.
Arguments:
- item_owner: int32 [4, 8, 128, 1], P('section', 'dp'), may hold values from 0 to 7; in each aligned block of 128 rows (0 to 127, 128 to 255, ..., all dimensions but the last counted through in order) at most 32 rows name the same one
- item_row: int32 [4, 8, 128], P('section', 'dp'), may hold values from 0 to 255
- lengths: int32 [4, 8], P(None, 'dp'), may hold values from 1 to 128
- table: bfloat16 [2048, 1024], P('dp'), may hold values from -6 to 6
- w_in: bfloat16 [4, 1024, 4096], P('section', 'dp'), may hold values from -0.1875 to 0.1875
- w_out: bfloat16 [4, 1024, 1024], P('section', 'dp'), may hold values from -0.1875 to 0.1875
- gain_in: float32 [4, 1024], P('section'), may hold values from 0.5 to 1.5
- gain_mid: float32 [4, 1024], P('section'), may hold values from 0.5 to 1.5
Outputs:
- states: bfloat16 [4, 8, 4, 128, 1024], P('section', 'dp')
Inputs may be any that keep to these rules, and one draw needn't show every extreme that they name: Among the 128 events of one history no value of item_owner appears more than 32 times; some history reaches 32.
All inputs are finite; a program needn't handle non-finite values.
Results may differ from a plain program's by a relative error of at most 0.029.
Values may be sent and summed in bfloat16 or wider, within the bound.
A program may use at most 64 MiB of HBM per device.

v0:
```python
import jax
import jax.numpy as jnp
from jax import lax
from jax.sharding import PartitionSpec as P

HEADS = 8


EPS = 1e-05


def from_behind(block, axis, distance):
    devices = range(lax.axis_size(axis))
    route = [(i - distance, i) for i in devices if i - distance in devices]
    return lax.ppermute(block, axis, route)


def normalize(values):
    center = values - jnp.mean(values, axis=-1, keepdims=True)
    spread = jnp.mean(center * center, axis=-1, keepdims=True)
    return center * lax.rsqrt(spread + EPS)


def layer_part(current, length, weight_in, weight_out, scale_in, scale_mid):
    wide = current.astype(jnp.float32)
    normed = (normalize(wide) * scale_in).astype(jnp.bfloat16)
    uvqk = jax.nn.silu(jnp.dot(normed, weight_in, preferred_element_type=jnp.float32)).astype(
        jnp.bfloat16
    )
    u_part, v_part, q_part, k_part = jnp.split(uvqk, 4, axis=-1)
    rows = current.shape[0]
    head_width = current.shape[1] // HEADS
    position = jnp.arange(rows, dtype=jnp.int32)
    key_all, value_all = (k_part, v_part)
    key_ok = position >= 0
    count = key_all.shape[0]
    queries = q_part.reshape(rows, HEADS, head_width)
    keys = key_all.reshape(count, HEADS, head_width)
    values = value_all.reshape(count, HEADS, head_width)
    scores = jnp.einsum("qhd,khd->hqk", queries, keys, preferred_element_type=jnp.float32)
    allowed = (
        (position[None, :] <= position[:, None]) & (position[None, :] < length) & key_ok[None, :]
    )
    weights = jnp.where(
        allowed[None], jax.nn.silu(scores / jnp.sqrt(jnp.float32(head_width))), 0.0
    ).astype(jnp.bfloat16)
    attn = jnp.einsum("hqk,khd->qhd", weights, values, preferred_element_type=jnp.float32).reshape(
        rows, HEADS * head_width
    )
    mixed = (normalize(attn) * scale_mid * u_part.astype(jnp.float32)).astype(jnp.bfloat16)
    result = (jnp.dot(mixed, weight_out, preferred_element_type=jnp.float32) + wide).astype(
        jnp.bfloat16
    )
    return (result, k_part, v_part)


def lookup_items(item_owner, item_row, table):
    groups = lax.axis_size("dp")
    owner = item_owner.reshape(-1)
    rows = item_row.reshape(-1)
    seq_len = rows.shape[0]
    slots_each = max(2, 2 * seq_len // groups)
    match = (owner[:, None] == jnp.arange(groups, dtype=jnp.int32)[None, :]).astype(jnp.int32)
    earlier = jnp.cumsum(match, axis=0) - match
    slot = jnp.sum(earlier * match, axis=1)
    placed = match[:, :, None] * (
        slot[:, None, None] == jnp.arange(slots_each, dtype=jnp.int32)[None, None, :]
    ).astype(jnp.int32)
    request = jnp.sum(placed * (rows + 1)[:, None, None], axis=0) - 1
    received = lax.all_to_all(request, "dp", split_axis=0, concat_axis=0, tiled=True)
    found = jnp.take(table, jnp.maximum(received, 0), axis=0)
    found = jnp.where((received >= 0)[:, :, None], found, jnp.zeros_like(found))
    answered = lax.all_to_all(found, "dp", split_axis=0, concat_axis=0, tiled=True)
    flat_rows = answered.reshape(groups * slots_each, table.shape[1])
    return jnp.take(flat_rows, owner * slots_each + slot, axis=0)


def on_device(item_owner, item_row, lengths, table, w_in, w_out, gain_in, gain_mid):
    sections = lax.axis_size("section")
    here = lax.axis_index("section")
    micro = lengths.shape[0]
    lens = lengths[:, 0]
    embedded = lookup_items(item_owner, item_row, table)
    full_in, full_out = (
        lax.all_gather(w_in, "dp", axis=1, tiled=True),
        lax.all_gather(w_out, "dp", axis=1, tiled=True),
    )
    weight_in = full_in[0]
    weight_out = full_out[0]
    scale_in = gain_in[0]
    scale_mid = gain_mid[0]
    seq_len = embedded.shape[0]
    pieces = 1
    part_rows = seq_len // pieces
    ticks = pieces * micro + sections - 1
    blank = jnp.zeros((part_rows, embedded.shape[1]), jnp.bfloat16)

    def tick(step, carry):
        queue, incoming, kept_k, kept_v, saved = carry
        which = step - here
        valid = (which >= 0) & (which < pieces * micro)
        item = jnp.clip(which, 0, pieces * micro - 1)
        slot = item // pieces
        part = item % pieces
        offset = part * part_rows
        source = queue
        current = jnp.where(here == 0, source, incoming)
        length = lax.dynamic_index_in_dim(lens, slot, 0, keepdims=False)

        def work(block):
            return layer_part(block, length, weight_in, weight_out, scale_in, scale_mid)

        def skip(block):
            return (block, blank, blank)

        finished, new_k, new_v = lax.cond(valid, work, skip, current)
        first = valid & (part == 0)
        kept_k = jnp.where(first, new_k, kept_k)
        kept_v = jnp.where(first, new_v, kept_v)
        previous = lax.dynamic_slice(saved, (slot, offset, 0), (1, part_rows, embedded.shape[1]))
        saved = lax.dynamic_update_slice(
            saved, jnp.where(valid, finished[None], previous), (slot, offset, 0)
        )
        incoming = from_behind(finished, "section", 1)
        moved = from_behind(queue, "section", -1)
        queue = jnp.where(step % pieces == pieces - 1, moved, queue)
        return (queue, incoming, kept_k, kept_v, saved)

    start = (embedded, blank, blank, blank, jnp.zeros((micro,) + embedded.shape, jnp.bfloat16))
    queue, incoming, kept_k, kept_v, saved = lax.fori_loop(0, ticks, tick, start)
    return saved[None, None]


def solution(mesh):
    in_specs = (
        P("section", "dp", None, None),
        P("section", "dp", None),
        P(None, "dp"),
        P("dp", None),
        P("section", "dp", None),
        P("section", "dp", None),
        P("section", None),
        P("section", None),
    )
    out_specs = P("section", "dp", None, None, None)
    return jax.shard_map(
        on_device, mesh=mesh, in_specs=in_specs, out_specs=out_specs, check_vma=False
    )
```

profile of v0, /device:TPU:3, one launch (start us, length us, event | category | flops | bytes accessed | tf_op | source)
XLA Modules:
  0.0 365.9 jit_solution(12390380260293746640)
XLA Ops:
  10.7 10.7 %all_to_all.11 = s32[8,1,32]{2,1,0:T(1,128)S(1)} all-to-all(s32[8,1,32]{2,1,0:T(1,128)S(1)} %bitcast.74), channel_id=1, replica_groups=mesh['section'=4,'dp'=8] {'dp'}, dimensions={0} | all-to-all | bytes 2048 | tf_op jit(solution)/shard_map/all_to_all | solution.py:70
  23.6 3.5 all-to-all-start.1
  27.2 16.1 %all-to-all-done.1 = bf16[8,32,1024]{2,1,0:T(8,128)(2,1)S(1)} async-done(((bf16[8,32,1024]{2,1,0:T(8,128)(2,1)}), bf16[8,32,1024]{2,1,0:T(8,128)(2,1)S(1)}, u32[]{:S(2)}, u32[]{:S(2)}) %all-to-all-start.1) | async-done | bytes 524320 | tf_op jit(solution)/shard_map/all_to_all | solution.py:73
  44.9 17.3 %all-gather.5.cloned.1.call-done = bf16[1,1024,1024]{2,1,0:T(8,128)(2,1)} async-done(((bf16[1,128,1024]{2,1,0:T(8,128)(2,1)}), bf16[1,1024,1024]{2,1,0:T(8,128)(2,1)}) %all-gather.5.cloned.1.call-update) | async-done | bytes 2097168 | tf_op jit(solution)/shard_map/all_gather | solution.py:86
  62.3 126.3 %all-gather.3.cloned.1.call-done = bf16[1,1024,4096]{2,1,0:T(8,128)(2,1)} async-done(((bf16[1,128,4096]{2,1,0:T(8,128)(2,1)}), bf16[1,1024,4096]{2,1,0:T(8,128)(2,1)}) %all-gather.3.cloned.1.call-update) | async-done | bytes 8388624 | tf_op jit(solution)/shard_map/all_gather | solution.py:85
  189.7 169.3 %while.19 = (s32[]{:T(128)}, bf16[128,1024]{1,0:T(8,128)(2,1)}, bf16[128,1024]{1,0:T(8,128)(2,1)S(1)}, bf16[4,128,1024]{2,1,0:T(8,128)(2,1)}, s32[]{:T(128)}, /*...) while((s32[]{:T(128)}, bf16[128,1024]{1,0:T(8,128)(2,1)}, ...), condition=%wide.region_10.11_spmd, body=%wide.region_3.10_spmd.sunk | while | flops 1416266112 | bytes 38586588 | solution.py:130
  192.7 4.3 %collective-permute-start = (bf16[128,1024]{1,0:T(8,128)(2,1)}, bf16[128,1024]{1,0:T(8,128)(2,1)}, u32[]{:S(2)}, u32[]{:S(2)}) collective-permute-start(bf16[128,1024]{1,0:T(8,128)(2,1)} %copy-done.4), channel_id=1, source_target_pairs={{8,0},{16,8},{24,16},{9,1},{17,9},{25,17},{10,2},{18,10},{26,18},{... | collective-permute-start | bytes 786440 | tf_op jit(solution)/shard_map/while/body/eval_jaxpr/ppermute | solution.py:15
  197.0 1.7 fusion.49
  201.6 6.7 %collective-permute-start = (bf16[128,1024]{1,0:T(8,128)(2,1)}, bf16[128,1024]{1,0:T(8,128)(2,1)}, u32[]{:S(2)}, u32[]{:S(2)}) collective-permute-start(bf16[128,1024]{1,0:T(8,128)(2,1)} %copy-done.4), channel_id=1, source_target_pairs={{8,0},{16,8},{24,16},{9,1},{17,9},{25,17},{10,2},{18,10},{26,18},{... | collective-permute-start | bytes 786440 | tf_op jit(solution)/shard_map/while/body/eval_jaxpr/ppermute | solution.py:15
  208.4 1.7 fusion.49
  213.0 43.8 %collective-permute-start = (bf16[128,1024]{1,0:T(8,128)(2,1)}, bf16[128,1024]{1,0:T(8,128)(2,1)}, u32[]{:S(2)}, u32[]{:S(2)}) collective-permute-start(bf16[128,1024]{1,0:T(8,128)(2,1)} %copy-done.4), channel_id=1, source_target_pairs={{8,0},{16,8},{24,16},{9,1},{17,9},{25,17},{10,2},{18,10},{26,18},{... | collective-permute-start | bytes 786440 | tf_op jit(solution)/shard_map/while/body/eval_jaxpr/ppermute | solution.py:15
  256.9 1.7 fusion.49
  260.2 14.3 %conditional.2 = (bf16[128,1024]{1,0:T(8,128)(2,1)S(1)}) conditional(s32[]{:T(128)} %convert_element_type.84, bf16[128,1024]{1,0:T(8,128)(2,1)S(1)} %broadcast_select_fusion.3, (bf16[128,1024]{1,0:T(8,128)(2,1)S(1)}, f32[1,1024]{1,0:T(1,128)S(1)}, bf16[1024,4096]{1,0:T(8,128)(2,1)}, s32[4]{0:T(128)S(1)}, s32[]{:T(128)}, ...), branch_computations={%region_4.4_spmd, %region_5.9_spmd} | conditional | flops 1416003968 | bytes 33342828 | solution.py:116
  261.7 4.8 %multiply_convert_fusion = bf16[128,4096]{1,0:T(8,128)(2,1)S(1)} fusion(bf16[1024,4096]{1,0:T(8,128)(2,1)} %get-tuple-element.280, bf16[128,1024]{1,0:T(8,128)(2,1)S(1)} %get-tuple-element.278, f32[1024]{0:T(1024)S(1)} %bitcast.78, f32[128]{0:T(128)S(1)} %add_rsqrt_fusion.1, f32[128]{0:T(128)S(1)} %broadcast_multiply_fusion.1), kind=kOutput, calls=%fused_computation.2 | convolution fusion | flops 1077018624 | bytes 9704448 | tf_op jit(solution)/shard_map/while/body/eval_jaxpr/cond/branch_1_fun/dot_general | solution.py:27
  269.2 1.8 fusion.40
  275.9 6.9 %collective-permute-start = (bf16[128,1024]{1,0:T(8,128)(2,1)}, bf16[128,1024]{1,0:T(8,128)(2,1)}, u32[]{:S(2)}, u32[]{:S(2)}) collective-permute-start(bf16[128,1024]{1,0:T(8,128)(2,1)} %copy-done.4), channel_id=1, source_target_pairs={{8,0},{16,8},{24,16},{9,1},{17,9},{25,17},{10,2},{18,10},{26,18},{... | collective-permute-start | bytes 786440 | tf_op jit(solution)/shard_map/while/body/eval_jaxpr/ppermute | solution.py:15
  282.8 1.7 fusion.49
  286.2 14.3 %conditional.2 = (bf16[128,1024]{1,0:T(8,128)(2,1)S(1)}) conditional(s32[]{:T(128)} %convert_element_type.84, bf16[128,1024]{1,0:T(8,128)(2,1)S(1)} %broadcast_select_fusion.3, (bf16[128,1024]{1,0:T(8,128)(2,1)S(1)}, f32[1,1024]{1,0:T(1,128)S(1)}, bf16[1024,4096]{1,0:T(8,128)(2,1)}, s32[4]{0:T(128)S(1)}, s32[]{:T(128)}, ...), branch_computations={%region_4.4_spmd, %region_5.9_spmd} | conditional | flops 1416003968 | bytes 33342828 | solution.py:116
  287.7 4.8 %multiply_convert_fusion = bf16[128,4096]{1,0:T(8,128)(2,1)S(1)} fusion(bf16[1024,4096]{1,0:T(8,128)(2,1)} %get-tuple-element.280, bf16[128,1024]{1,0:T(8,128)(2,1)S(1)} %get-tuple-element.278, f32[1024]{0:T(1024)S(1)} %bitcast.78, f32[128]{0:T(128)S(1)} %add_rsqrt_fusion.1, f32[128]{0:T(128)S(1)} %broadcast_multiply_fusion.1), kind=kOutput, calls=%fused_computation.2 | convolution fusion | flops 1077018624 | bytes 9704448 | tf_op jit(solution)/shard_map/while/body/eval_jaxpr/cond/branch_1_fun/dot_general | solution.py:27
  295.2 1.8 fusion.40
  301.8 6.9 %collective-permute-start = (bf16[128,1024]{1,0:T(8,128)(2,1)}, bf16[128,1024]{1,0:T(8,128)(2,1)}, u32[]{:S(2)}, u32[]{:S(2)}) collective-permute-start(bf16[128,1024]{1,0:T(8,128)(2,1)} %copy-done.4), channel_id=1, source_target_pairs={{8,0},{16,8},{24,16},{9,1},{17,9},{25,17},{10,2},{18,10},{26,18},{... | collective-permute-start | bytes 786440 | tf_op jit(solution)/shard_map/while/body/eval_jaxpr/ppermute | solution.py:15
  308.7 1.7 fusion.49
  312.1 14.3 %conditional.2 = (bf16[128,1024]{1,0:T(8,128)(2,1)S(1)}) conditional(s32[]{:T(128)} %convert_element_type.84, bf16[128,1024]{1,0:T(8,128)(2,1)S(1)} %broadcast_select_fusion.3, (bf16[128,1024]{1,0:T(8,128)(2,1)S(1)}, f32[1,1024]{1,0:T(1,128)S(1)}, bf16[1024,4096]{1,0:T(8,128)(2,1)}, s32[4]{0:T(128)S(1)}, s32[]{:T(128)}, ...), branch_computations={%region_4.4_spmd, %region_5.9_spmd} | conditional | flops 1416003968 | bytes 33342828 | solution.py:116
  313.5 4.8 %multiply_convert_fusion = bf16[128,4096]{1,0:T(8,128)(2,1)S(1)} fusion(bf16[1024,4096]{1,0:T(8,128)(2,1)} %get-tuple-element.280, bf16[128,1024]{1,0:T(8,128)(2,1)S(1)} %get-tuple-element.278, f32[1024]{0:T(1024)S(1)} %bitcast.78, f32[128]{0:T(128)S(1)} %add_rsqrt_fusion.1, f32[128]{0:T(128)S(1)} %broadcast_multiply_fusion.1), kind=kOutput, calls=%fused_computation.2 | convolution fusion | flops 1077018624 | bytes 9704448 | tf_op jit(solution)/shard_map/while/body/eval_jaxpr/cond/branch_1_fun/dot_general | solution.py:27
  321.0 1.8 fusion.40
  327.7 6.9 %collective-permute-start = (bf16[128,1024]{1,0:T(8,128)(2,1)}, bf16[128,1024]{1,0:T(8,128)(2,1)}, u32[]{:S(2)}, u32[]{:S(2)}) collective-permute-start(bf16[128,1024]{1,0:T(8,128)(2,1)} %copy-done.4), channel_id=1, source_target_pairs={{8,0},{16,8},{24,16},{9,1},{17,9},{25,17},{10,2},{18,10},{26,18},{... | collective-permute-start | bytes 786440 | tf_op jit(solution)/shard_map/while/body/eval_jaxpr/ppermute | solution.py:15
  334.6 1.7 fusion.49
  338.0 14.3 %conditional.2 = (bf16[128,1024]{1,0:T(8,128)(2,1)S(1)}) conditional(s32[]{:T(128)} %convert_element_type.84, bf16[128,1024]{1,0:T(8,128)(2,1)S(1)} %broadcast_select_fusion.3, (bf16[128,1024]{1,0:T(8,128)(2,1)S(1)}, f32[1,1024]{1,0:T(1,128)S(1)}, bf16[1024,4096]{1,0:T(8,128)(2,1)}, s32[4]{0:T(128)S(1)}, s32[]{:T(128)}, ...), branch_computations={%region_4.4_spmd, %region_5.9_spmd} | conditional | flops 1416003968 | bytes 33342828 | solution.py:116
  339.4 4.8 %multiply_convert_fusion = bf16[128,4096]{1,0:T(8,128)(2,1)S(1)} fusion(bf16[1024,4096]{1,0:T(8,128)(2,1)} %get-tuple-element.280, bf16[128,1024]{1,0:T(8,128)(2,1)S(1)} %get-tuple-element.278, f32[1024]{0:T(1024)S(1)} %bitcast.78, f32[128]{0:T(128)S(1)} %add_rsqrt_fusion.1, f32[128]{0:T(128)S(1)} %broadcast_multiply_fusion.1), kind=kOutput, calls=%fused_computation.2 | convolution fusion | flops 1077018624 | bytes 9704448 | tf_op jit(solution)/shard_map/while/body/eval_jaxpr/cond/branch_1_fun/dot_general | solution.py:27
  346.9 1.8 fusion.40
  353.6 3.7 %collective-permute-start = (bf16[128,1024]{1,0:T(8,128)(2,1)}, bf16[128,1024]{1,0:T(8,128)(2,1)}, u32[]{:S(2)}, u32[]{:S(2)}) collective-permute-start(bf16[128,1024]{1,0:T(8,128)(2,1)} %copy-done.4), channel_id=1, source_target_pairs={{8,0},{16,8},{24,16},{9,1},{17,9},{25,17},{10,2},{18,10},{26,18},{... | collective-permute-start | bytes 786440 | tf_op jit(solution)/shard_map/while/body/eval_jaxpr/ppermute | solution.py:15
  357.3 1.7 fusion.49
  (167 shorter events, 60.1 us)
Async XLA Ops:
  6.5 15.0 %copy-start = (bf16[256,1024]{1,0:T(8,128)(2,1)S(1)}, bf16[256,1024]{1,0:T(8,128)(2,1)}, u32[]{:S(2)}) copy-start(bf16[256,1024]{1,0:T(8,128)(2,1)} %param.15) | copy-start | bytes 1572868
  6.5 55.7 %all-gather.5.cloned.1.call-start = ((), (), s32[]{:S(2)}) async-start(), calls=%async_computation.3 | async-start | bytes 2359296 | tf_op jit(solution)/shard_map/all_gather | solution.py:86
  7.3 181.3 %all-gather.3.cloned.1.call-start = ((), (), s32[]{:S(2)}) async-start(), calls=%async_computation.2 | async-start | bytes 9437184 | tf_op jit(solution)/shard_map/all_gather | solution.py:85
  22.7 4.5 %copy-start.6 = (s32[1,1,128,1]{2,3,1,0:T(1,128)S(1)}, s32[1,1,128,1]{2,3,1,0:T(1,128)}, u32[]{:S(2)}) copy-start(s32[1,1,128,1]{2,3,1,0:T(1,128)} %param.12) | copy-start | bytes 1540
  23.6 19.6 %all-to-all-start.1 = ((bf16[8,32,1024]{2,1,0:T(8,128)(2,1)}), bf16[8,32,1024]{2,1,0:T(8,128)(2,1)S(1)}, u32[]{:S(2)}, u32[]{:S(2)}) async-start(bf16[8,32,1024]{2,1,0:T(8,128)(2,1)} %select_select_fusion), calls=%async_computation.1 | async-start | bytes 1048576 | tf_op jit(solution)/shard_map/all_to_all | solution.py:73
  43.3 146.4 %copy-start.5 = (f32[1,1024]{1,0:T(1,128)S(1)}, f32[1,1024]{1,0:T(1,128)}, u32[]{:S(2)}) copy-start(f32[1,1024]{1,0:T(1,128)} %param.19) | copy-start | bytes 12292
  43.3 146.4 %copy-start.7 = (f32[1,1024]{1,0:T(1,128)S(1)}, f32[1,1024]{1,0:T(1,128)}, u32[]{:S(2)}) copy-start(f32[1,1024]{1,0:T(1,128)} %param.18) | copy-start | bytes 12292
  43.3 146.4 %copy-start.8 = (s32[4,1]{0,1:T(1,128)S(1)}, s32[4,1]{0,1:T(1,128)}, u32[]{:S(2)}) copy-start(s32[4,1]{0,1:T(1,128)} %param.14) | copy-start | bytes 52
  191.4 7.3 %collective-permute-start.1 = (bf16[128,1024]{1,0:T(8,128)(2,1)S(1)}, bf16[128,1024]{1,0:T(8,128)(2,1)S(1)}, u32[]{:S(2)}, u32[]{:S(2)}) collective-permute-start(bf16[128,1024]{1,0:T(8,128)(2,1)S(1)} %get-tuple-element.440), channel_id=1, source_target_pairs={{0,8},{8,16},{16,24},{1,9},{9,17},{17,25},{2,10},{10,18},{18,26},{... | collective-permute-start | bytes 786440 | tf_op jit(solution)/shard_map/while/body/eval_jaxpr/ppermute | solution.py:15
  192.7 6.0 %collective-permute-start = (bf16[128,1024]{1,0:T(8,128)(2,1)}, bf16[128,1024]{1,0:T(8,128)(2,1)}, u32[]{:S(2)}, u32[]{:S(2)}) collective-permute-start(bf16[128,1024]{1,0:T(8,128)(2,1)} %copy-done.4), channel_id=1, source_target_pairs={{8,0},{16,8},{24,16},{9,1},{17,9},{25,17},{10,2},{18,10},{26,18},{... | collective-permute-start | bytes 786440 | tf_op jit(solution)/shard_map/while/body/eval_jaxpr/ppermute | solution.py:15
  200.3 9.7 %collective-permute-start.1 = (bf16[128,1024]{1,0:T(8,128)(2,1)S(1)}, bf16[128,1024]{1,0:T(8,128)(2,1)S(1)}, u32[]{:S(2)}, u32[]{:S(2)}) collective-permute-start(bf16[128,1024]{1,0:T(8,128)(2,1)S(1)} %get-tuple-element.440), channel_id=1, source_target_pairs={{0,8},{8,16},{16,24},{1,9},{9,17},{17,25},{2,10},{10,18},{18,26},{... | collective-permute-start | bytes 786440 | tf_op jit(solution)/shard_map/while/body/eval_jaxpr/ppermute | solution.py:15
  201.6 8.5 %collective-permute-start = (bf16[128,1024]{1,0:T(8,128)(2,1)}, bf16[128,1024]{1,0:T(8,128)(2,1)}, u32[]{:S(2)}, u32[]{:S(2)}) collective-permute-start(bf16[128,1024]{1,0:T(8,128)(2,1)} %copy-done.4), channel_id=1, source_target_pairs={{8,0},{16,8},{24,16},{9,1},{17,9},{25,17},{10,2},{18,10},{26,18},{... | collective-permute-start | bytes 786440 | tf_op jit(solution)/shard_map/while/body/eval_jaxpr/ppermute | solution.py:15
  211.7 46.8 %collective-permute-start.1 = (bf16[128,1024]{1,0:T(8,128)(2,1)S(1)}, bf16[128,1024]{1,0:T(8,128)(2,1)S(1)}, u32[]{:S(2)}, u32[]{:S(2)}) collective-permute-start(bf16[128,1024]{1,0:T(8,128)(2,1)S(1)} %get-tuple-element.440), channel_id=1, source_target_pairs={{0,8},{8,16},{16,24},{1,9},{9,17},{17,25},{2,10},{10,18},{18,26},{... | collective-permute-start | bytes 786440 | tf_op jit(solution)/shard_map/while/body/eval_jaxpr/ppermute | solution.py:15
  213.0 45.6 %collective-permute-start = (bf16[128,1024]{1,0:T(8,128)(2,1)}, bf16[128,1024]{1,0:T(8,128)(2,1)}, u32[]{:S(2)}, u32[]{:S(2)}) collective-permute-start(bf16[128,1024]{1,0:T(8,128)(2,1)} %copy-done.4), channel_id=1, source_target_pairs={{8,0},{16,8},{24,16},{9,1},{17,9},{25,17},{10,2},{18,10},{26,18},{... | collective-permute-start | bytes 786440 | tf_op jit(solution)/shard_map/while/body/eval_jaxpr/ppermute | solution.py:15
  266.6 1.0 copy-start.3
  269.2 3.9 %copy-start.1 = (bf16[1024,1024]{1,0:T(8,128)(2,1)S(1)}, bf16[1024,1024]{1,0:T(8,128)(2,1)}, u32[]{:S(2)}) copy-start(bf16[1024,1024]{1,0:T(8,128)(2,1)} %get-tuple-element.284) | copy-start | bytes 6291460 | tf_op jit(solution)/shard_map/while/body/eval_jaxpr/cond
  271.0 0.8 copy-start.2
  274.6 10.0 %collective-permute-start.1 = (bf16[128,1024]{1,0:T(8,128)(2,1)S(1)}, bf16[128,1024]{1,0:T(8,128)(2,1)S(1)}, u32[]{:S(2)}, u32[]{:S(2)}) collective-permute-start(bf16[128,1024]{1,0:T(8,128)(2,1)S(1)} %get-tuple-element.440), channel_id=1, source_target_pairs={{0,8},{8,16},{16,24},{1,9},{9,17},{17,25},{2,10},{10,18},{18,26},{... | collective-permute-start | bytes 786440 | tf_op jit(solution)/shard_map/while/body/eval_jaxpr/ppermute | solution.py:15
  275.9 8.7 %collective-permute-start = (bf16[128,1024]{1,0:T(8,128)(2,1)}, bf16[128,1024]{1,0:T(8,128)(2,1)}, u32[]{:S(2)}, u32[]{:S(2)}) collective-permute-start(bf16[128,1024]{1,0:T(8,128)(2,1)} %copy-done.4), channel_id=1, source_target_pairs={{8,0},{16,8},{24,16},{9,1},{17,9},{25,17},{10,2},{18,10},{26,18},{... | collective-permute-start | bytes 786440 | tf_op jit(solution)/shard_map/while/body/eval_jaxpr/ppermute | solution.py:15
  292.5 1.0 copy-start.3
  295.2 3.9 %copy-start.1 = (bf16[1024,1024]{1,0:T(8,128)(2,1)S(1)}, bf16[1024,1024]{1,0:T(8,128)(2,1)}, u32[]{:S(2)}) copy-start(bf16[1024,1024]{1,0:T(8,128)(2,1)} %get-tuple-element.284) | copy-start | bytes 6291460 | tf_op jit(solution)/shard_map/while/body/eval_jaxpr/cond
  297.0 0.8 copy-start.2
  300.5 9.9 %collective-permute-start.1 = (bf16[128,1024]{1,0:T(8,128)(2,1)S(1)}, bf16[128,1024]{1,0:T(8,128)(2,1)S(1)}, u32[]{:S(2)}, u32[]{:S(2)}) collective-permute-start(bf16[128,1024]{1,0:T(8,128)(2,1)S(1)} %get-tuple-element.440), channel_id=1, source_target_pairs={{0,8},{8,16},{16,24},{1,9},{9,17},{17,25},{2,10},{10,18},{18,26},{... | collective-permute-start | bytes 786440 | tf_op jit(solution)/shard_map/while/body/eval_jaxpr/ppermute | solution.py:15
  301.8 8.6 %collective-permute-start = (bf16[128,1024]{1,0:T(8,128)(2,1)}, bf16[128,1024]{1,0:T(8,128)(2,1)}, u32[]{:S(2)}, u32[]{:S(2)}) collective-permute-start(bf16[128,1024]{1,0:T(8,128)(2,1)} %copy-done.4), channel_id=1, source_target_pairs={{8,0},{16,8},{24,16},{9,1},{17,9},{25,17},{10,2},{18,10},{26,18},{... | collective-permute-start | bytes 786440 | tf_op jit(solution)/shard_map/while/body/eval_jaxpr/ppermute | solution.py:15
  318.4 1.0 copy-start.3
  321.0 3.9 %copy-start.1 = (bf16[1024,1024]{1,0:T(8,128)(2,1)S(1)}, bf16[1024,1024]{1,0:T(8,128)(2,1)}, u32[]{:S(2)}) copy-start(bf16[1024,1024]{1,0:T(8,128)(2,1)} %get-tuple-element.284) | copy-start | bytes 6291460 | tf_op jit(solution)/shard_map/while/body/eval_jaxpr/cond
  326.4 9.9 %collective-permute-start.1 = (bf16[128,1024]{1,0:T(8,128)(2,1)S(1)}, bf16[128,1024]{1,0:T(8,128)(2,1)S(1)}, u32[]{:S(2)}, u32[]{:S(2)}) collective-permute-start(bf16[128,1024]{1,0:T(8,128)(2,1)S(1)} %get-tuple-element.440), channel_id=1, source_target_pairs={{0,8},{8,16},{16,24},{1,9},{9,17},{17,25},{2,10},{10,18},{18,26},{... | collective-permute-start | bytes 786440 | tf_op jit(solution)/shard_map/while/body/eval_jaxpr/ppermute | solution.py:15
  327.7 8.6 %collective-permute-start = (bf16[128,1024]{1,0:T(8,128)(2,1)}, bf16[128,1024]{1,0:T(8,128)(2,1)}, u32[]{:S(2)}, u32[]{:S(2)}) collective-permute-start(bf16[128,1024]{1,0:T(8,128)(2,1)} %copy-done.4), channel_id=1, source_target_pairs={{8,0},{16,8},{24,16},{9,1},{17,9},{25,17},{10,2},{18,10},{26,18},{... | collective-permute-start | bytes 786440 | tf_op jit(solution)/shard_map/while/body/eval_jaxpr/ppermute | solution.py:15
  344.3 1.0 copy-start.3
  346.9 3.9 %copy-start.1 = (bf16[1024,1024]{1,0:T(8,128)(2,1)S(1)}, bf16[1024,1024]{1,0:T(8,128)(2,1)}, u32[]{:S(2)}) copy-start(bf16[1024,1024]{1,0:T(8,128)(2,1)} %get-tuple-element.284) | copy-start | bytes 6291460 | tf_op jit(solution)/shard_map/while/body/eval_jaxpr/cond
  352.3 6.8 %collective-permute-start.1 = (bf16[128,1024]{1,0:T(8,128)(2,1)S(1)}, bf16[128,1024]{1,0:T(8,128)(2,1)S(1)}, u32[]{:S(2)}, u32[]{:S(2)}) collective-permute-start(bf16[128,1024]{1,0:T(8,128)(2,1)S(1)} %get-tuple-element.440), channel_id=1, source_target_pairs={{0,8},{8,16},{16,24},{1,9},{9,17},{17,25},{2,10},{10,18},{18,26},{... | collective-permute-start | bytes 786440 | tf_op jit(solution)/shard_map/while/body/eval_jaxpr/ppermute | solution.py:15
  353.6 5.5 %collective-permute-start = (bf16[128,1024]{1,0:T(8,128)(2,1)}, bf16[128,1024]{1,0:T(8,128)(2,1)}, u32[]{:S(2)}, u32[]{:S(2)}) collective-permute-start(bf16[128,1024]{1,0:T(8,128)(2,1)} %copy-done.4), channel_id=1, source_target_pairs={{8,0},{16,8},{24,16},{9,1},{17,9},{25,17},{10,2},{18,10},{26,18},{... | collective-permute-start | bytes 786440 | tf_op jit(solution)/shard_map/while/body/eval_jaxpr/ppermute | solution.py:15
  (9 other events, 6.4 us)
Sparse Core Ops, SparseCore 0:
  9.5 52.7 all-gather.4
  64.4 124.1 all-gather.2
where the time goes:
time: 371 us; the launch traced here: 366 us
  waiting for transfers between devices  161 us (43%)
  starting transfers between devices  91.9 us (25%)
  local copies, waits for them, and re-layouts  34.8 us (9%)
  matrix products  32.4 us (9%)
  other arithmetic  21.1 us (6%)
  between operations  13.5 us (4%)
  blocking collectives  10.7 us (3%)
    all_gather x1, waiting for transfers between devices, on_device(): lax.all_gather(w_in, 'dp', axis=1, tiled=True)  126 us
    ppermute x14, starting transfers between devices, from_behind(): return lax.ppermute(block, axis, route)  88.4 us
    dot_general x4, matrix products, layer_part(): jnp.dot(normed, weight_in, preferred_element_type=jnp.float32)  19.3 us
    all_gather x1, waiting for transfers between devices, on_device(): lax.all_gather(w_out, 'dp', axis=1, tiled=True)  17.3 us
    all_to_all x1, waiting for transfers between devices, lookup_items(): lax.all_to_all(found, 'dp', split_axis=0, concat_axis=0, tiled=True)  16.1 us
    dynamic_update_slice x7, other arithmetic, tick(): lax.dynamic_update_slice(saved, jnp.where(valid, finished[None], previous...  12 us
    all_to_all x1, blocking collectives, lookup_items(): lax.all_to_all(request, 'dp', split_axis=0, concat_axis=0, tiled=True)  10.7 us
    cond x28, local copies, waits for them, and re-layouts  9.65 us
  transfers between devices with their start and end apart: 17, of which 3 were waited for; matrix products, arithmetic and copies ran while one was open for 5% of the time, Pallas kernels for 0%

commit v1 on v0

v1 whole, which is shorter than its diff:
```python
import functools

import jax
import jax.numpy as jnp
from jax import lax
from jax.experimental import pallas as pl
from jax.experimental.pallas import tpu as pltpu
from jax.sharding import PartitionSpec as P

HEADS = 8
EPS = 1e-05
MESH = pl.DeviceIdType.MESH
SUBLANES = 8
PACKED_ROWS = 16


def dot(a, b, contract=(1, 0)):
    dims = (((contract[0],), (contract[1],)), ((), ()))
    return lax.dot_general(a, b, dims, preferred_element_type=jnp.float32)


def silu(v):
    half = 0.5 * v
    return half + half * jnp.tanh(half)


def normalize(values):
    center = values - jnp.mean(values, axis=-1, keepdims=True)
    spread = jnp.mean(center * center, axis=-1, keepdims=True)
    return center * lax.rsqrt(spread + EPS)


def kernel(
    lines,
    lens_ref, code_ref, table_ref, w_in_ref, w_out_ref, gain_in_ref, gain_mid_ref,
    out_ref,
    win, wout, codes, answers, found, staged, xin, normed, uvqk, attn,
    local_sem, win_send, win_recv, wout_send, wout_recv,
    code_send, code_recv, found_send, found_recv, x_send, x_recv, next_send,
):
    major, minor = lines
    groups = major * minor
    here, me = lax.axis_index("section"), lax.axis_index("dp")
    sections = lax.axis_size("section")
    a, b = me // minor, me % minor
    depth, depth_out = w_in_ref.shape[0], w_out_ref.shape[0]
    micro, seq, width = xin.shape
    cap = answers.shape[1]
    items = table_ref.shape[0]
    head = width // HEADS

    def rows(ref, block, count):
        return ref.at[pl.ds(pl.multiple_of(block * count, count), count)]

    def target(kind):
        if kind == 0:
            return (a + 1) * minor + b
        if kind == 1:
            return (a - 1) * minor + b
        return a * minor + (b + kind - 1) % minor

    def weight_copy(which, block, kind):
        full, send, recv, count = (
            (win, win_send, win_recv, depth) if which == 0 else (wout, wout_send, wout_recv, depth_out)
        )
        part = rows(full, block, count)
        return pltpu.make_async_remote_copy(
            src_ref=part, dst_ref=part, send_sem=send.at[block, kind], recv_sem=recv.at[block],
            device_id={"dp": target(kind)}, device_id_type=MESH,
        )

    def code_copy(block, to):
        return pltpu.make_async_remote_copy(
            src_ref=codes.at[block], dst_ref=codes.at[block], send_sem=code_send.at[to],
            recv_sem=code_recv.at[block], device_id={"dp": to}, device_id_type=MESH,
        )

    def found_copy(to, block):
        return pltpu.make_async_remote_copy(
            src_ref=answers.at[to], dst_ref=found.at[block], send_sem=found_send.at[to],
            recv_sem=found_recv.at[block], device_id={"dp": to}, device_id_type=MESH,
        )

    def to_first(slot):
        return pltpu.make_async_remote_copy(
            src_ref=staged, dst_ref=xin.at[slot], send_sem=x_send.at[0], recv_sem=x_recv.at[slot],
            device_id={"section": 0}, device_id_type=MESH,
        )

    def to_next(slot):
        return pltpu.make_async_remote_copy(
            src_ref=out_ref.at[slot], dst_ref=xin.at[slot], send_sem=next_send.at[slot],
            recv_sem=x_recv.at[slot], device_id={"section": here + 1}, device_id_type=MESH,
        )

    UP, DOWN = 0, 1
    ACROSS = range(2, minor + 1)

    def other(off):
        return a * minor + (b + off) % minor

    def start_if(copy, condition):
        if condition is None:
            copy.start()
        else:
            pl.when(condition)(copy.start)

    own_in = pltpu.make_async_copy(w_in_ref, rows(win, me, depth), local_sem.at[0])
    own_out = pltpu.make_async_copy(w_out_ref, rows(wout, me, depth_out), local_sem.at[1])
    own_in.start()
    own_out.start()
    codes[me] = jnp.broadcast_to(code_ref[...], codes.shape[1:])

    def send_code(off, _):
        code_copy(me, lax.rem(me + off, groups)).start()
        return 0

    lax.fori_loop(1, groups, send_code, 0)
    own_out.wait()
    own_in.wait()
    for which in (1, 0):
        for kind in ACROSS:
            weight_copy(which, me, kind).start()
        start_if(weight_copy(which, me, UP), a < major - 1)
        start_if(weight_copy(which, me, DOWN), a > 0)

    before = (
        lax.broadcasted_iota(jnp.int32, (seq, seq), 0) < lax.broadcasted_iota(jnp.int32, (seq, seq), 1)
    ).astype(jnp.float32).astype(jnp.bfloat16)

    def ranks(code, owner):
        local = code - owner * items
        mine = (local >= 0) & (local < items)
        flag = jnp.where(mine, 1.0, 0.0)
        rank = dot(flag.astype(jnp.bfloat16), before).astype(jnp.int32)
        return local, mine, rank

    def one_hot(keys, count):
        spot = lax.broadcasted_iota(jnp.int32, (count, seq), 0)
        return jnp.where(spot == keys, 1.0, 0.0)

    def answer(to):
        local, mine, rank = ranks(codes[to], me)
        slot = jnp.where(mine, rank, -1)
        pick_slot = one_hot(slot[:1], cap).astype(jnp.bfloat16)
        pick_row = one_hot(local[:1], items).astype(jnp.bfloat16)
        pick = dot(pick_slot, pick_row, (1, 1)).astype(jnp.bfloat16)
        return dot(pick, table_ref[...]).astype(jnp.bfloat16)

    found[me] = answer(me)

    def send_answer(off, _):
        to = lax.rem(me + off, groups)
        code_copy(to, to).wait_recv()
        answers[to] = answer(to)
        found_copy(to, me).start()
        return 0

    lax.fori_loop(1, groups, send_answer, 0)

    for off in range(1, minor):
        spot = other(off)
        weight_copy(1, spot, UP).wait_recv()
        start_if(weight_copy(1, spot, UP), a < major - 1)
        start_if(weight_copy(1, spot, DOWN), a > 0)

    for step in range(1, major):
        for sign, kind, inside, onward in (
            (-1, UP, a - step >= 0, a < major - 1),
            (1, DOWN, a + step < major, a > 0),
        ):
            @pl.when(inside)
            def _():
                for off in range(minor):
                    spot = (a + sign * step) * minor + (b + off) % minor
                    weight_copy(1, spot, kind).wait_recv()
                    start_if(weight_copy(1, spot, kind), onward)
                spot = (a + sign * step) * minor + b
                weight_copy(0, spot, kind).wait_recv()
                start_if(weight_copy(0, spot, kind), onward)
                for across in ACROSS:
                    weight_copy(0, spot, across).start()

    def key_of(owner, keys):
        _, mine, rank = ranks(codes[me], owner)
        return jnp.where(mine, owner * cap + rank, keys)

    keys = lax.fori_loop(0, groups, key_of, jnp.zeros((SUBLANES, seq), jnp.int32))
    place = one_hot(keys[:1], groups * cap).T.astype(jnp.bfloat16)

    def wait_found(off, _):
        source = lax.rem(me + off, groups)
        found_copy(source, source).wait_recv()
        return 0

    lax.fori_loop(1, groups, wait_found, 0)
    embedded = dot(place, found[...].reshape(groups * cap, width)).astype(jnp.bfloat16)

    @pl.when(here == 0)
    def _():
        xin[0] = embedded

    @pl.when(here > 0)
    def _():
        staged[...] = embedded
        to_first(here).start()

    for off in range(1, minor):
        for line in range(major):
            weight_copy(0, line * minor + (b + off) % minor, 1 + off).wait_recv()

    later = lax.broadcasted_iota(jnp.int32, (seq, seq), 1)
    causal = later <= lax.broadcasted_iota(jnp.int32, (seq, seq), 0)

    def layer(slot, _):
        @pl.when((here > 0) | (slot > 0))
        def _():
            to_first(slot).wait_recv()

        wide = xin[slot].astype(jnp.float32)
        normed[...] = (normalize(wide) * gain_in_ref[...]).astype(jnp.bfloat16)
        for tile in range(4 * width // (4 * head)):
            columns = slice(tile * 4 * head, (tile + 1) * 4 * head)
            uvqk[:, columns] = silu(dot(normed[...], win[:, columns])).astype(jnp.bfloat16)
        allowed = causal & (later < lens_ref[slot, 0])
        for h in range(HEADS):
            part = [slice(k * width + h * head, k * width + (h + 1) * head) for k in range(4)]
            scores = dot(uvqk[:, part[2]], uvqk[:, part[3]], (1, 1)) * (head**-0.5)
            weights = jnp.where(allowed, silu(scores), 0.0).astype(jnp.bfloat16)
            attn[:, part[0]] = dot(weights, uvqk[:, part[1]])
        mixed = normalize(attn[...]) * gain_mid_ref[...] * uvqk[:, :width].astype(jnp.float32)
        normed[...] = mixed.astype(jnp.bfloat16)
        out_ref[slot] = (dot(normed[...], wout[...]) + xin[slot].astype(jnp.float32)).astype(jnp.bfloat16)

        @pl.when(here < sections - 1)
        def _():
            to_next(slot).start()

        return 0

    lax.fori_loop(0, micro, layer, 0)

    def left(off, _):
        to = lax.rem(me + off, groups)
        code_copy(me, to).wait_send()
        found_copy(to, me).wait_send()
        return 0

    lax.fori_loop(1, groups, left, 0)
    for which in (1, 0):
        for kind in ACROSS:
            weight_copy(which, me, kind).wait_send()
    for off in range(minor):
        for which in (1, 0) if off == 0 else (1,):
            copies = [weight_copy(which, other(off), kind) for kind in (UP, DOWN)]
            pl.when(a < major - 1)(copies[0].wait_send)
            pl.when(a > 0)(copies[1].wait_send)
    for step in range(1, major):
        for sign, kind, inside, onward in (
            (-1, UP, a - step >= 0, a < major - 1),
            (1, DOWN, a + step < major, a > 0),
        ):
            @pl.when(inside)
            def _():
                for off in range(minor):
                    spot = (a + sign * step) * minor + (b + off) % minor
                    pl.when(onward)(weight_copy(1, spot, kind).wait_send)
                spot = (a + sign * step) * minor + b
                pl.when(onward)(weight_copy(0, spot, kind).wait_send)
                for across in ACROSS:
                    weight_copy(0, spot, across).wait_send()

    pl.when(here > 0)(to_first(here).wait_send)

    def passed(slot, _):
        pl.when(here < sections - 1)(to_next(slot).wait_send)
        return 0

    lax.fori_loop(0, micro, passed, 0)


def on_device(lines, item_owner, item_row, lengths, table, w_in, w_out, gain_in, gain_mid):
    major, minor = lines
    groups = major * minor
    items, width = table.shape
    seq = item_row.shape[-1]
    micro = lengths.shape[0]
    cap = max(PACKED_ROWS, 2 * seq // groups)
    code = item_owner.reshape(1, seq) * items + item_row.reshape(1, seq)
    inner = w_in.shape[1] * groups
    vmem = pl.BlockSpec(memory_space=pltpu.VMEM)
    hbm = pl.BlockSpec(memory_space=pl.ANY)
    smem = pl.BlockSpec(memory_space=pltpu.SMEM)
    dma = pltpu.SemaphoreType.DMA
    kinds = minor + 1
    bf16 = jnp.bfloat16
    out = pl.pallas_call(
        functools.partial(kernel, lines),
        out_shape=jax.ShapeDtypeStruct((micro, seq, width), bf16),
        in_specs=[smem, vmem, vmem, hbm, hbm, vmem, vmem],
        out_specs=vmem,
        scratch_shapes=[
            pltpu.VMEM((inner, w_in.shape[2]), bf16),
            pltpu.VMEM((w_out.shape[1] * groups, width), bf16),
            pltpu.VMEM((groups, SUBLANES, seq), jnp.int32),
            pltpu.VMEM((groups, cap, width), bf16),
            pltpu.VMEM((groups, cap, width), bf16),
            pltpu.VMEM((seq, width), bf16),
            pltpu.VMEM((micro, seq, width), bf16),
            pltpu.VMEM((seq, width), bf16),
            pltpu.VMEM((seq, w_in.shape[2]), bf16),
            pltpu.VMEM((seq, width), jnp.float32),
            dma((2,)),
            dma((groups, kinds)),
            dma((groups,)),
            dma((groups, kinds)),
            dma((groups,)),
            dma((groups,)),
            dma((groups,)),
            dma((groups,)),
            dma((groups,)),
            dma((1,)),
            dma((micro,)),
            dma((micro,)),
        ],
        compiler_params=pltpu.CompilerParams(
            has_side_effects=True, vmem_limit_bytes=40 * 2**20
        ),
        name="sections",
    )(lengths, code, table, w_in[0], w_out[0], gain_in, gain_mid)
    return out[None, None]


def lines_of(mesh):
    along = [device.coords for device in mesh.devices[0]]
    moved = [[axis for axis in range(3) if along[0][axis] != spot[axis]] for spot in along]
    minor = 1
    while minor < len(along) and moved[minor] == moved[1] and len(moved[1]) == 1:
        minor += 1
    return len(along) // minor, minor


def solution(mesh):
    in_specs = (
        P("section", "dp", None, None),
        P("section", "dp", None),
        P(None, "dp"),
        P("dp", None),
        P("section", "dp", None),
        P("section", "dp", None),
        P("section", None),
        P("section", None),
    )
    out_specs = P("section", "dp", None, None, None)
    return jax.shard_map(
        functools.partial(on_device, lines_of(mesh)),
        mesh=mesh, in_specs=in_specs, out_specs=out_specs, check_vma=False,
    )
```

time: 371 us -> 182 us (0.49); the launches traced: 366 us -> 181 us
  Pallas kernels: 0 us -> 176 us
  waiting for transfers between devices: 161 us -> 0 us
  starting transfers between devices: 91.9 us -> 0 us
  matrix products: 32.4 us -> 0 us
  local copies, waits for them, and re-layouts: 34.8 us -> 4.94 us
  other arithmetic: 21.1 us -> 0.7 us
  between operations: 13.5 us -> 0.02 us
  blocking collectives: 10.7 us -> 0 us
    pallas_call x0 -> x1, Pallas kernels: none -> 176 us  [on_device(): pl.pallas_call(functools.partial(kernel, lines), out_shape=jax.ShapeDtype...]
    all_gather x2 -> x0, waiting for transfers between devices: 144 us -> none  [the longest x1 126 us: on_device(): lax.all_gather(w_in, 'dp', axis=1, tiled=True)]
    ppermute x14 -> x0, starting transfers between devices: 88.4 us -> none  [from_behind(): return lax.ppermute(block, axis, route)]
    dot_general x12 -> x0, matrix products: 32.4 us -> none  [the longest x4 19.3 us: layer_part(): jnp.dot(normed, weight_in, preferred_element_type=jnp.float32)]
    all_to_all x1 -> x0, waiting for transfers between devices: 16.1 us -> none  [lookup_items(): lax.all_to_all(found, 'dp', split_axis=0, concat_axis=0, tiled=True)]
    dynamic_update_slice x7 -> x0, other arithmetic: 12 us -> none  [tick(): lax.dynamic_update_slice(saved, jnp.where(valid, finished[None], previous...]
    all_to_all x1 -> x0, blocking collectives: 10.7 us -> none  [lookup_items(): lax.all_to_all(request, 'dp', split_axis=0, concat_axis=0, tiled=True)]
    cond x28 -> x0, local copies, waits for them, and re-layouts: 9.65 us -> none
  transfers between devices with their start and end apart: 17 -> 0, of which waited for: 3 -> 0; matrix products, arithmetic and copies ran while one was open for 5% -> 0% of each run, Pallas kernels for 0% -> 0%
where the time goes in v1:
time: 182 us; the launch traced here: 181 us
  Pallas kernels  176 us (97%)
  local copies, waits for them, and re-layouts  4.94 us (3%)
    pallas_call x1, Pallas kernels, on_device(): pl.pallas_call(functools.partial(kernel, lines), out_shape=jax.ShapeDtype...  176 us
    unnamed x12, local copies, waits for them, and re-layouts  4.94 us

profile of v1, /device:TPU:3, one launch (start us, length us, event | category | flops | bytes accessed | tf_op | source)
XLA Modules:
  0.0 181.3 jit_solution(9486760699910715253)
XLA Ops:
  0.0 0.0 copy-start.4
  0.0 0.0 copy-start.3
  0.0 0.7 bitcast_add_fusion.code_ref
  0.7 0.7 copy.9.lens_ref
  1.4 0.0 copy-done.4
  1.5 0.0 copy-done.3
  1.5 0.0 copy-start
  1.5 1.2 copy-done
  2.7 0.0 copy-start.1
  2.7 1.0 copy-done.1
  3.7 0.0 copy-start.2
  3.7 0.9 copy-done.2
  4.7 175.6 %sections.1 = bf16[4,128,1024]{2,1,0:T(8,128)(2,1)S(1)} custom-call(s32[4,1]{1,0:T(4,128)S(1)} %copy.9.lens_ref, s32[1,128]{1,0:T(1,128)S(1)} %bitcast_add_fusion.code_ref, bf16[256,1024]{1,0:T(8,128)(2,1)S(1)} %copy-done.1, bf16[128,4096]{1,0:T(8,128)(2,1)S(1)} %bitcast.8, bf16[128,1024]{1,0:T(8,128)(2,1)S(1)} %bitcast.9, f32[1,1024]{1,0:T(1,128)S(1)} %copy-done.3, ...), custom_call_target="tpu_custom_call" | custom-call | tf_op jit(solution)/shard_map/sections/pallas_call | solution.py:297
  180.3 1.0 copy.11
Async XLA Ops:
  0.0 1.4 copy-start.4
  0.0 1.4 copy-start.3
  1.5 1.2 copy-start
  2.7 1.0 copy-start.1
  3.7 0.9 copy-start.2

commit v2 on v1

--- a/solution.py
+++ b/solution.py
@@ -47,6 +47,7 @@
     micro, seq, width = xin.shape
     cap = answers.shape[1]
     items = table_ref.shape[0]
+    pieces = win_recv.shape[0] // groups
     head = width // HEADS
 
     def rows(ref, block, count):
@@ -59,13 +60,16 @@
             return (a - 1) * minor + b
         return a * minor + (b + kind - 1) % minor
 
-    def weight_copy(which, block, kind):
+    def weight_copy(which, block, kind, piece=0):
         full, send, recv, count = (
-            (win, win_send, win_recv, depth) if which == 0 else (wout, wout_send, wout_recv, depth_out)
-        )
-        part = rows(full, block, count)
-        return pltpu.make_async_remote_copy(
-            src_ref=part, dst_ref=part, send_sem=send.at[block, kind], recv_sem=recv.at[block],
+            (win, win_send, win_recv, depth // pieces)
+            if which == 0
+            else (wout, wout_send, wout_recv, depth_out)
+        )
+        spot = block * pieces + piece if which == 0 else block
+        part = rows(full, spot, count)
+        return pltpu.make_async_remote_copy(
+            src_ref=part, dst_ref=part, send_sem=send.at[spot, kind], recv_sem=recv.at[spot],
             device_id={"dp": target(kind)}, device_id_type=MESH,
         )
 
@@ -118,11 +122,19 @@
     lax.fori_loop(1, groups, send_code, 0)
     own_out.wait()
     own_in.wait()
-    for which in (1, 0):
+    for kind in ACROSS:
+        weight_copy(1, me, kind).start()
+    start_if(weight_copy(1, me, UP), a < major - 1)
+    start_if(weight_copy(1, me, DOWN), a > 0)
+
+    def send_own(piece, _):
+        start_if(weight_copy(0, me, UP, piece), a < major - 1)
+        start_if(weight_copy(0, me, DOWN, piece), a > 0)
         for kind in ACROSS:
-            weight_copy(which, me, kind).start()
-        start_if(weight_copy(which, me, UP), a < major - 1)
-        start_if(weight_copy(which, me, DOWN), a > 0)
+            weight_copy(0, me, kind, piece).start()
+        return 0
+
+    lax.fori_loop(0, pieces, send_own, 0)
 
     before = (
         lax.broadcasted_iota(jnp.int32, (seq, seq), 0) < lax.broadcasted_iota(jnp.int32, (seq, seq), 1)
@@ -164,22 +176,34 @@
         start_if(weight_copy(1, spot, UP), a < major - 1)
         start_if(weight_copy(1, spot, DOWN), a > 0)
 
+    def sides(step):
+        return (
+            (-step, UP, a - step >= 0, a < major - 1),
+            (step, DOWN, a + step < major, a > 0),
+        )
+
     for step in range(1, major):
-        for sign, kind, inside, onward in (
-            (-1, UP, a - step >= 0, a < major - 1),
-            (1, DOWN, a + step < major, a > 0),
-        ):
+        for shift, kind, inside, onward in sides(step):
             @pl.when(inside)
             def _():
                 for off in range(minor):
-                    spot = (a + sign * step) * minor + (b + off) % minor
+                    spot = (a + shift) * minor + (b + off) % minor
                     weight_copy(1, spot, kind).wait_recv()
                     start_if(weight_copy(1, spot, kind), onward)
-                spot = (a + sign * step) * minor + b
-                weight_copy(0, spot, kind).wait_recv()
-                start_if(weight_copy(0, spot, kind), onward)
-                for across in ACROSS:
-                    weight_copy(0, spot, across).start()
+
+        def relay(piece, _):
+            for shift, kind, inside, onward in sides(step):
+                @pl.when(inside)
+                def _():
+                    spot = (a + shift) * minor + b
+                    weight_copy(0, spot, kind, piece).wait_recv()
+                    start_if(weight_copy(0, spot, kind, piece), onward)
+                    for across in ACROSS:
+                        weight_copy(0, spot, across, piece).start()
+
+            return 0
+
+        lax.fori_loop(0, pieces, relay, 0)
 
     def key_of(owner, keys):
         _, mine, rank = ranks(codes[me], owner)
@@ -206,8 +230,12 @@
         to_first(here).start()
 
     for off in range(1, minor):
-        for line in range(major):
-            weight_copy(0, line * minor + (b + off) % minor, 1 + off).wait_recv()
+        def arrived(count, _):
+            line, piece = count // pieces, count % pieces
+            weight_copy(0, line * minor + (b + off) % minor, 1 + off, piece).wait_recv()
+            return 0
+
+        lax.fori_loop(0, major * pieces, arrived, 0)
 
     later = lax.broadcasted_iota(jnp.int32, (seq, seq), 1)
     causal = later <= lax.broadcasted_iota(jnp.int32, (seq, seq), 0)
@@ -247,28 +275,36 @@
         return 0
 
     lax.fori_loop(1, groups, left, 0)
-    for which in (1, 0):
+    for kind in ACROSS:
+        weight_copy(1, me, kind).wait_send()
+    for off in range(minor):
+        pl.when(a < major - 1)(weight_copy(1, other(off), UP).wait_send)
+        pl.when(a > 0)(weight_copy(1, other(off), DOWN).wait_send)
+
+    def own_left(piece, _):
+        pl.when(a < major - 1)(weight_copy(0, me, UP, piece).wait_send)
+        pl.when(a > 0)(weight_copy(0, me, DOWN, piece).wait_send)
         for kind in ACROSS:
-            weight_copy(which, me, kind).wait_send()
-    for off in range(minor):
-        for which in (1, 0) if off == 0 else (1,):
-            copies = [weight_copy(which, other(off), kind) for kind in (UP, DOWN)]
-            pl.when(a < major - 1)(copies[0].wait_send)
-            pl.when(a > 0)(copies[1].wait_send)
+            weight_copy(0, me, kind, piece).wait_send()
+        return 0
+
+    lax.fori_loop(0, pieces, own_left, 0)
     for step in range(1, major):
-        for sign, kind, inside, onward in (
-            (-1, UP, a - step >= 0, a < major - 1),
-            (1, DOWN, a + step < major, a > 0),
-        ):
+        for shift, kind, inside, onward in sides(step):
             @pl.when(inside)
             def _():
                 for off in range(minor):
-                    spot = (a + sign * step) * minor + (b + off) % minor
+                    spot = (a + shift) * minor + (b + off) % minor
                     pl.when(onward)(weight_copy(1, spot, kind).wait_send)
-                spot = (a + sign * step) * minor + b
-                pl.when(onward)(weight_copy(0, spot, kind).wait_send)
-                for across in ACROSS:
-                    weight_copy(0, spot, across).wait_send()
+
+                def relay_left(piece, _):
+                    spot = (a + shift) * minor + b
+                    pl.when(onward)(weight_copy(0, spot, kind, piece).wait_send)
+                    for across in ACROSS:
+                        weight_copy(0, spot, across, piece).wait_send()
+                    return 0
+
+                lax.fori_loop(0, pieces, relay_left, 0)
 
     pl.when(here > 0)(to_first(here).wait_send)
 
@@ -293,6 +329,7 @@
     smem = pl.BlockSpec(memory_space=pltpu.SMEM)
     dma = pltpu.SemaphoreType.DMA
     kinds = minor + 1
+    pieces = max(1, w_in.shape[1] // (2 * PACKED_ROWS))
     bf16 = jnp.bfloat16
     out = pl.pallas_call(
         functools.partial(kernel, lines),
@@ -311,8 +348,8 @@
             pltpu.VMEM((seq, w_in.shape[2]), bf16),
             pltpu.VMEM((seq, width), jnp.float32),
             dma((2,)),
-            dma((groups, kinds)),
-            dma((groups,)),
+            dma((groups * pieces, kinds)),
+            dma((groups * pieces,)),
             dma((groups, kinds)),
             dma((groups,)),
             dma((groups,)),

time: 182 us -> 166 us (0.912)
  Pallas kernels: 176 us -> 160 us
    pallas_call x1, Pallas kernels: 176 us -> 160 us  [on_device(): pl.pallas_call(functools.partial(kernel, lines), out_shape=jax.ShapeDtype...]
where the time goes in v2:
time: 166 us; the launch traced here: 165 us
  Pallas kernels  160 us (96%)
  local copies, waits for them, and re-layouts  4.94 us (3%)
    pallas_call x1, Pallas kernels, on_device(): pl.pallas_call(functools.partial(kernel, lines), out_shape=jax.ShapeDtype...  160 us
    unnamed x12, local copies, waits for them, and re-layouts  4.94 us

profile of v2, /device:TPU:3, one launch (start us, length us, event | category | flops | bytes accessed | tf_op | source)
XLA Modules:
  0.0 165.4 jit_solution(11810209708207910313)
XLA Ops:
  0.0 0.0 copy-start.4
  0.0 0.0 copy-start.3
  0.0 0.7 bitcast_add_fusion.code_ref
  0.7 0.7 copy.9.lens_ref
  1.4 0.0 copy-done.4
  1.5 0.0 copy-done.3
  1.5 0.0 copy-start
  1.5 1.2 copy-done
  2.7 0.0 copy-start.1
  2.7 1.0 copy-done.1
  3.7 0.0 copy-start.2
  3.7 0.9 copy-done.2
  4.7 159.8 %sections.1 = bf16[4,128,1024]{2,1,0:T(8,128)(2,1)S(1)} custom-call(s32[4,1]{1,0:T(4,128)S(1)} %copy.9.lens_ref, s32[1,128]{1,0:T(1,128)S(1)} %bitcast_add_fusion.code_ref, bf16[256,1024]{1,0:T(8,128)(2,1)S(1)} %copy-done.1, bf16[128,4096]{1,0:T(8,128)(2,1)S(1)} %bitcast.8, bf16[128,1024]{1,0:T(8,128)(2,1)S(1)} %bitcast.9, f32[1,1024]{1,0:T(1,128)S(1)} %copy-done.3, ...), custom_call_target="tpu_custom_call" | custom-call | tf_op jit(solution)/shard_map/sections/pallas_call | solution.py:334
  164.4 1.0 copy.11
Async XLA Ops:
  0.0 1.4 copy-start.4
  0.0 1.4 copy-start.3
  1.5 1.2 copy-start
  2.7 1.0 copy-start.1
  3.7 0.9 copy-start.2

commit v3 on v2

--- a/solution.py
+++ b/solution.py
@@ -124,8 +124,6 @@
     own_in.wait()
     for kind in ACROSS:
         weight_copy(1, me, kind).start()
-    start_if(weight_copy(1, me, UP), a < major - 1)
-    start_if(weight_copy(1, me, DOWN), a > 0)
 
     def send_own(piece, _):
         start_if(weight_copy(0, me, UP, piece), a < major - 1)
@@ -135,6 +133,8 @@
         return 0
 
     lax.fori_loop(0, pieces, send_own, 0)
+    start_if(weight_copy(1, me, UP), a < major - 1)
+    start_if(weight_copy(1, me, DOWN), a > 0)
 
     before = (
         lax.broadcasted_iota(jnp.int32, (seq, seq), 0) < lax.broadcasted_iota(jnp.int32, (seq, seq), 1)
@@ -183,14 +183,6 @@
         )
 
     for step in range(1, major):
-        for shift, kind, inside, onward in sides(step):
-            @pl.when(inside)
-            def _():
-                for off in range(minor):
-                    spot = (a + shift) * minor + (b + off) % minor
-                    weight_copy(1, spot, kind).wait_recv()
-                    start_if(weight_copy(1, spot, kind), onward)
-
         def relay(piece, _):
             for shift, kind, inside, onward in sides(step):
                 @pl.when(inside)
@@ -204,6 +196,13 @@
             return 0
 
         lax.fori_loop(0, pieces, relay, 0)
+        for shift, kind, inside, onward in sides(step):
+            @pl.when(inside)
+            def _():
+                for off in range(minor):
+                    spot = (a + shift) * minor + (b + off) % minor
+                    weight_copy(1, spot, kind).wait_recv()
+                    start_if(weight_copy(1, spot, kind), onward)
 
     def key_of(owner, keys):
         _, mine, rank = ranks(codes[me], owner)

time: 166 us -> 160 us (0.964)
  Pallas kernels: 160 us -> 154 us
    pallas_call x1, Pallas kernels: 160 us -> 154 us  [on_device(): pl.pallas_call(functools.partial(kernel, lines), out_shape=jax.ShapeDtype...]
where the time goes in v3:
time: 160 us
  Pallas kernels  154 us (96%)
  local copies, waits for them, and re-layouts  4.94 us (3%)
    pallas_call x1, Pallas kernels, on_device(): pl.pallas_call(functools.partial(kernel, lines), out_shape=jax.ShapeDtype...  154 us
    unnamed x12, local copies, waits for them, and re-layouts  4.94 us

profile of v3, /device:TPU:3, one launch (start us, length us, event | category | flops | bytes accessed | tf_op | source)
XLA Modules:
  0.0 160.0 jit_solution(15894432701168701115)
XLA Ops:
  0.0 0.0 copy-start.4
  0.0 0.0 copy-start.3
  0.0 0.7 bitcast_add_fusion.code_ref
  0.7 0.7 copy.9.lens_ref
  1.4 0.0 copy-done.4
  1.5 0.0 copy-done.3
  1.5 0.0 copy-start
  1.5 1.2 copy-done
  2.7 0.0 copy-start.1
  2.7 1.0 copy-done.1
  3.7 0.0 copy-start.2
  3.7 0.9 copy-done.2
  4.7 154.3 %sections.1 = bf16[4,128,1024]{2,1,0:T(8,128)(2,1)S(1)} custom-call(s32[4,1]{1,0:T(4,128)S(1)} %copy.9.lens_ref, s32[1,128]{1,0:T(1,128)S(1)} %bitcast_add_fusion.code_ref, bf16[256,1024]{1,0:T(8,128)(2,1)S(1)} %copy-done.1, bf16[128,4096]{1,0:T(8,128)(2,1)S(1)} %bitcast.8, bf16[128,1024]{1,0:T(8,128)(2,1)S(1)} %bitcast.9, f32[1,1024]{1,0:T(1,128)S(1)} %copy-done.3, ...), custom_call_target="tpu_custom_call" | custom-call | tf_op jit(solution)/shard_map/sections/pallas_call | solution.py:333
  159.0 1.0 copy.11
Async XLA Ops:
  0.0 1.4 copy-start.4
  0.0 1.4 copy-start.3
  1.5 1.2 copy-start
  2.7 1.0 copy-start.1
  3.7 0.9 copy-start.2
